TPU v7x, 32 devices: a whole 2x2x4 slice. The times are simulated.
32 devices in a mesh: dp: 8 (over z, x), tensor: 4 (over y, core).
Axes of the slice: x: 2, y: 2, z: 4, core: 2. Of those that a mesh axis runs over, the one named last changes fastest.
Arguments:
- tokens: bfloat16 [16384, 768], P(('dp', 'tensor')), may hold values from -6 to 6
- segment: int32 [16384], P(('dp', 'tensor')), may hold values from 0 to 512, as said below
- live: int32 [16384], P(('dp', 'tensor')), may hold values from 0 to 1, as said below
- mix_weight: bfloat16 [3, 768, 768], replicated, may hold values from -0.21875 to 0.21875
- out_weight: bfloat16 [768, 768], replicated, may hold values from -0.875 to 0.875
- position_table: bfloat16 [512, 768], replicated, may hold values from -6 to 6
- norm_gain: float32 [2, 768], replicated, may hold values from 0.5 to 1.5
- norm_bias: float32 [2, 768], replicated, may hold values from -1.5 to 1.5
- mix_left: bfloat16 [4, 768, 12], replicated, may hold values from -0.21875 to 0.21875
- mix_scale: float32 [4, 12], replicated, may hold values from -3 to 3
- mix_right: bfloat16 [4, 12, 768], replicated, may hold values from -1.75 to 1.75
- expand_weight: bfloat16 [768, 3072], P(None, 'tensor'), may hold values from -0.21875 to 0.21875
- expand_left: bfloat16 [768, 12], replicated, may hold values from -0.21875 to 0.21875
- expand_right: bfloat16 [12, 3072], P(None, 'tensor'), may hold values from -1.75 to 1.75
- shrink_weight: bfloat16 [3072, 768], P('tensor'), may hold values from -0.21875 to 0.21875
- shrink_left: bfloat16 [3072, 12], P('tensor'), may hold values from -0.21875 to 0.21875
- feed_scale: float32 [2, 12], replicated, may hold values from -3 to 3
- shrink_right: bfloat16 [12, 768], replicated, may hold values from -1.75 to 1.75
- cotangent: bfloat16 [16384, 768], P(('dp', 'tensor'))
Outputs:
- layer_out: bfloat16 [16384, 768], P(('dp', 'tensor'))
- grad_tokens: float32 [16384, 768], P(('dp', 'tensor'))
- grad_mix_left: float32 [4, 768, 12], replicated
- grad_mix_scale: float32 [4, 12], replicated
- grad_mix_right: float32 [4, 12, 768], replicated
- grad_expand_left: float32 [768, 12], replicated
- grad_expand_right: float32 [12, 3072], P(None, 'tensor')
- grad_shrink_left: float32 [3072, 12], P('tensor')
- grad_feed_scale: float32 [2, 12], replicated
- grad_shrink_right: float32 [12, 768], replicated
Inputs may be any that keep to these rules, and one draw needn't show every extreme that they name: `segment`: within each aligned block of 512 slots (one device's slots) the live slots come first and their sequence numbers start at 0 and never fall; padding slots carry 512; some block holds a single sequence of 512 tokens. In each aligned block of 512 slots the live ones come first, at least 256 of them; some block is fully live.
All inputs are finite; a program needn't handle non-finite values.
Results may differ from a plain program's by a relative error of at most 0.023.
Values may be sent and summed in bfloat16 or wider, within the bound.
A program may use at most 192 MiB of HBM per device.

v0:
```python
import math

import jax
import jax.numpy as jnp
from jax import lax
from jax.experimental import pallas as pl
from jax.experimental.pallas import tpu as pltpu
from jax.sharding import PartitionSpec as P

PAIRS = 6
LANES = 128
ROWS = 512
WIDTH = 768
RANK = 12
BLOCKS = ROWS // LANES
TILE = 16
GROUP = 2
BACK_GROUP = 4
STACK = 64
SPLIT_AT = 25

norm_eps = 1e-07
masked_fill = -1e30
score_scale = 1.0 / math.sqrt(192.0)
inverse_root_two = 1.0 / math.sqrt(2.0)
log_two_e = math.log2(math.e)
inverse_root_tau = 1.0 / math.sqrt(2.0 * math.pi)

f32 = jnp.float32
bf16 = jnp.bfloat16


def dot_nn(left, right):
    return jnp.dot(left, right, preferred_element_type=f32)


def dot_nt(left, right):
    return lax.dot_general(left, right, (((1,), (1,)), ((), ())), preferred_element_type=f32)


def dot_tn(left, right):
    return lax.dot_general(left, right, (((0,), (0,)), ((), ())), preferred_element_type=f32)


def column_of(row):
    n = row.shape[1]
    eye = lax.broadcasted_iota(jnp.int32, (n, n), 0) == lax.broadcasted_iota(jnp.int32, (n, n), 1)
    return jnp.sum(jnp.where(eye, row, 0.0), axis=1, keepdims=True)


def spread(scale):
    row = lax.broadcasted_iota(jnp.int32, (RANK, STACK), 0)
    lane = lax.broadcasted_iota(jnp.int32, (RANK, STACK), 1)
    total = jnp.zeros((1, STACK), f32)
    for a in range(4):
        column = column_of(scale[a : a + 1, :])
        total = total + jnp.sum(
            jnp.where(lane == row + TILE * a, column, 0.0), axis=0, keepdims=True
        )
    return total


def of_map(which):
    lane = lax.broadcasted_iota(jnp.int32, (1, STACK), 1)
    return (lane // TILE == which).astype(bf16)


def block_iotas():
    shape = (LANES, LANES)
    return lax.broadcasted_iota(jnp.int32, shape, 0), lax.broadcasted_iota(jnp.int32, shape, 1)


def head_mask(which):
    lane = lax.broadcasted_iota(jnp.int32, (1, LANES), 1)
    return ((lane >= 64) if which else (lane < 64)).astype(bf16)


def pick_tiles(scores, block, at_diag):
    first = scores[:, :1]
    last = scores[:, ROWS - 1 :]
    near = {}

    def rolled(u):
        if u not in near:
            near[u] = pltpu.roll(
                scores[:, u * LANES : (u + 1) * LANES], 1, 1, stride=1, stride_axis=0
            )
        return near[u]

    tiles = []
    for other in range(BLOCKS):
        v = other - block + 2
        if v < 0:
            tile = jnp.broadcast_to(first, (LANES, LANES))
        elif v == 0:
            tile = jnp.where(at_diag, first, rolled(0))
        elif v < 4:
            tile = jnp.where(at_diag, rolled(v - 1), rolled(v))
        elif v == 4:
            tile = jnp.where(at_diag, rolled(3), last)
        else:
            tile = jnp.broadcast_to(last, (LANES, LANES))
        tiles.append(tile)
    return jnp.concatenate(tiles, axis=1)


def row_sums(values):
    part = (
        values[:, :LANES]
        + values[:, LANES : 2 * LANES]
        + values[:, 2 * LANES : 3 * LANES]
        + values[:, 3 * LANES :]
    )
    high = part.astype(bf16)
    rest = (part - high.astype(f32)).astype(bf16)
    return dot_nn(jnp.concatenate([high, rest], axis=1), jnp.ones((2 * LANES, LANES), bf16))


def wide4(values):
    return jnp.concatenate([values] * BLOCKS, axis=1)


def fold_rows(grads, block, beyond, inside, pick_first, pick_last):
    zero = jnp.zeros((LANES, LANES), f32)
    near = {}
    low = []
    high = []
    for other in range(BLOCKS):
        v = other - block + 2
        tile = grads[:, other * LANES : (other + 1) * LANES]
        if v < 0:
            low.append(tile.astype(bf16))
        elif v > 4:
            high.append(tile.astype(bf16))
        else:
            near[v] = pltpu.roll(tile, 0, 1, stride=1, stride_axis=0)
        if v == 0:
            low.append(tile.astype(bf16) * inside)
        if v == 4:
            high.append(tile.astype(bf16) * (1 - inside))
    out = []
    for w in range(BLOCKS):
        if w in near or w + 1 in near:
            out.append(jnp.where(beyond, near.get(w + 1, zero), near.get(w, zero)))
        else:
            out.append(zero)
    if low:
        out[0] = out[0] + dot_nn(
            jnp.concatenate(low, axis=1), pick_first[: LANES * len(low), :]
        )
    if high:
        out[3] = out[3] + dot_nn(
            jnp.concatenate(high, axis=1), pick_last[: LANES * len(high), :]
        )
    return jnp.concatenate(out, axis=1)


def attend_part(
    segment,
    live,
    tokens,
    table,
    mix_weight,
    mix_copies,
    left_s,
    right_s,
    scale_row,
    rank_s,
    table_rank_s,
    shares_out,
    q_s,
    k_s,
    v_s,
    tq_s,
    tk_s,
    tr_s,
    context_s,
    shares_s,
    bias_s,
    across_s,
    work,
    sems,
    gather,
):
    row, lane = block_iotas()
    below = lane <= row
    flip = (row + lane == LANES - 1).astype(bf16)
    eye = (row == lane).astype(bf16)
    seg_row = segment[...]
    key_row = jnp.where(live[...] == 1, seg_row, -1)
    for a in range(BLOCKS):
        seg_col = jnp.broadcast_to(
            seg_row[:, a * LANES : (a + 1) * LANES].astype(f32), (LANES, LANES)
        ).T.astype(jnp.int32)
        for b in range(BLOCKS):
            same = seg_col == key_row[:, b * LANES : (b + 1) * LANES]
            if a == b:
                same = same | (row == lane)
            bias_s[a * LANES : (a + 1) * LANES, b * LANES : (b + 1) * LANES] = jnp.where(
                same, 0.0, masked_fill
            )
    for a in range(BLOCKS):
        tr_s[a * LANES : (a + 1) * LANES, :] = dot_nn(
            flip, table[(3 - a) * LANES : (4 - a) * LANES, :]
        ).astype(bf16)

    rank_s[...] = dot_nt(tokens[...], left_s[...])
    table_rank_s[...] = dot_nt(tr_s[...], left_s[...])
    low = (rank_s[...] * scale_row).astype(bf16)
    table_low = (table_rank_s[...] * scale_row).astype(bf16)

    def project(source, low, which, target):
        full = dot_nn(source, mix_weight[which]) + dot_nn(low * of_map(which), right_s[...])
        for p in range(PAIRS):
            target[p] = full[:, p * LANES : (p + 1) * LANES].astype(bf16)

    mix_copies[0].wait()
    project(tokens[...], low, 0, q_s)
    project(tr_s[...], table_low, 0, tq_s)
    mix_copies[1].wait()
    project(tokens[...], low, 1, k_s)
    project(tr_s[...], table_low, 1, tk_s)
    gather.forward_one(0)
    mix_copies[2].wait()
    project(tokens[...], low, 2, v_s)

    blocks = [slice(b * LANES, (b + 1) * LANES) for b in range(BLOCKS)]
    keys_s, queries_s, along_s, both_s = work[:4]
    context_part = work[4]

    def scores(p, which):
        mask = head_mask(which)
        keys_s[which][:, :ROWS] = dot_nt(k_s[p] * mask, tq_s[p])
        queries_s[which][:, :ROWS] = dot_nt(q_s[p] * mask, tk_s[p])

    def pick(p, which):
        for b, r in enumerate(blocks):
            values = pick_tiles(keys_s[which][r, :ROWS], b, below)
            high = values.astype(bf16)
            across_s[which, 0, r, :] = high
            across_s[which, 1, r, :] = (values - high.astype(f32)).astype(bf16)
            along_s[which][r, :ROWS] = pick_tiles(queries_s[which][r, :ROWS], b, below)

    def content(p, which):
        mask = head_mask(which)
        for r in blocks:
            both_s[which][r, :ROWS] = dot_nt(
                jnp.concatenate([q_s[p, r, :] * mask, eye, eye], axis=1),
                jnp.concatenate(
                    [k_s[p], across_s[which, 0, :, r], across_s[which, 1, :, r]], axis=1
                ),
            )

    def softmax(p, which):
        for first in range(0, BLOCKS, GROUP):
            rows = blocks[first : first + GROUP]
            totals = [
                both_s[which][r, :ROWS] + along_s[which][r, :ROWS] + bias_s[r, :] for r in rows
            ]
            peaks = [jnp.max(t, axis=1, keepdims=True) for t in totals]
            weights = [
                jnp.exp2((t - m) * (score_scale * log_two_e)) for t, m in zip(totals, peaks)
            ]
            inverses = [1.0 / jnp.sum(w, axis=1, keepdims=True) for w in weights]
            for r, w, inverse in zip(rows, weights, inverses):
                shares_s[p, which, r, :] = (w * inverse).astype(bf16)

    def mix(p, which):
        part = dot_nn(shares_s[p, which], v_s[p] * head_mask(which))
        if which == 0:
            context_part[:, :LANES] = part
        else:
            lanes = slice(p * LANES, (p + 1) * LANES)
            if not isinstance(p, int):
                lanes = pl.ds(pl.multiple_of(p * LANES, LANES), LANES)
            context_s[:, lanes] = (context_part[:, :LANES] + part).astype(bf16)

    stages = (mix, softmax, content, pick, scores)

    def step(base, extra, first=0, last=4):
        for n in range(first, last + 1):
            head = extra - (4 - n)
            stages[n](base + head // 2, head % 2)

    def give(p):
        pltpu.make_async_copy(shares_s.at[p], shares_out.at[p], sems.at[p]).start()

    for extra in range(4):
        if extra == 2:
            gather.forward_one(1)
        step(0, extra, first=4 - extra)

    def pair(base, carry):
        for at, forward, k in (
            (2, gather.forward_one, 2),
            (3, gather.forward_two, 0),
            (4, gather.forward_one, 3),
            (5, gather.forward_two, 1),
        ):

            @pl.when(base == at)
            def _():
                forward(k)

        step(base, 0)
        step(base, 1)
        give(base - 2)
        return carry

    lax.fori_loop(2, PAIRS, pair, 0)
    gather.forward_one(4)
    step(PAIRS, 0, last=3)
    gather.forward_two(2)
    step(PAIRS, 1, last=2)
    give(PAIRS - 2)
    step(PAIRS, 2, last=1)
    gather.forward_two(3)
    give(PAIRS - 1)
    step(PAIRS, 3, last=0)


def vmem():
    return pl.BlockSpec(memory_space=pltpu.VMEM)


def anywhere():
    return pl.BlockSpec(memory_space=pl.ANY)


def remote(source, target, send, recv, device):
    return pltpu.make_async_remote_copy(
        src_ref=source,
        dst_ref=target,
        send_sem=send,
        recv_sem=recv,
        device_id=device,
        device_id_type=pl.DeviceIdType.MESH,
    )


def greet(devices):
    barrier = pltpu.get_barrier_semaphore()
    for device in devices:
        pl.semaphore_signal(
            barrier, inc=1, device_id=device, device_id_type=pl.DeviceIdType.MESH
        )
    pl.semaphore_wait(barrier, len(devices))


class Groups:
    def __init__(self, tensor_size, dp_size):
        self.near_size = tensor_size * 2
        self.far_size = dp_size // 2
        self.tensor = lax.axis_index("tensor")
        self.dp = lax.axis_index("dp")
        self.near = self.tensor * 2 + self.dp % 2
        self.far = self.dp // 2

    def near_index(self, step):
        return (self.near + step) % self.near_size

    def near_device(self, step):
        index = self.near_index(step)
        return {"dp": self.far * 2 + index % 2, "tensor": index // 2}

    def far_device(self, step):
        index = (self.far + step) % self.far_size
        return {"dp": index * 2 + self.dp % 2, "tensor": self.tensor}

    def partners(self):
        return [self.near_device(s) for s in range(1, self.near_size)] + [
            self.far_device(s) for s in range(1, self.far_size)
        ]


class Reduction:
    def __init__(self, groups, pack, arrived, crossed, out, sems):
        self.groups = groups
        self.pack = pack
        self.arrived = arrived
        self.crossed = crossed
        self.out = out
        self.send_one, self.recv_one, self.send_two, self.recv_two, self.send_three, self.recv_three = sems
        self.size = pack.shape[0] // groups.near_size

    def part(self, ref, index):
        return ref.at[pl.ds(index * self.size, self.size)]

    def scatter(self):
        g = self.groups
        return [
            remote(
                self.part(self.pack, g.near_index(s)),
                self.arrived.at[s - 1],
                self.send_one.at[s - 1],
                self.recv_one.at[s - 1],
                g.near_device(s),
            )
            for s in range(1, g.near_size)
        ]

    def cross(self):
        g = self.groups
        return [
            remote(
                self.crossed.at[g.far],
                self.crossed.at[g.far],
                self.send_two.at[s - 1],
                self.recv_two.at[s - 1],
                g.far_device(s),
            )
            for s in range(1, g.far_size)
        ]

    def gather(self):
        g = self.groups
        return [
            remote(
                self.part(self.out, g.near),
                self.part(self.out, g.near),
                self.send_three.at[s - 1],
                self.recv_three.at[s - 1],
                g.near_device(s),
            )
            for s in range(1, g.near_size)
        ]

    def start(self):
        for copy in self.scatter():
            copy.start()

    def middle(self):
        g = self.groups
        for copy in self.scatter():
            copy.wait()
        total = self.pack[pl.ds(g.near * self.size, self.size)].astype(f32)
        for s in range(1, g.near_size):
            total = total + self.arrived[s - 1].astype(f32)
        self.crossed[g.far] = total.astype(self.crossed.dtype)
        for copy in self.cross():
            copy.start()

    def last(self):
        g = self.groups
        for copy in self.cross():
            copy.wait()
        total = self.crossed[0].astype(f32)
        for s in range(1, g.far_size):
            total = total + self.crossed[s].astype(f32)
        self.out[pl.ds(g.near * self.size, self.size)] = total.astype(self.out.dtype)
        for copy in self.gather():
            copy.start()

    def finish(self):
        for copy in self.gather():
            copy.wait()


def reduction_scratch(tiles, near_size, far_size, kind):
    size = tiles // near_size
    near = (near_size - 1,)
    far = (max(far_size - 1, 1),)
    dma = pltpu.SemaphoreType.DMA
    return [
        pltpu.VMEM((near_size - 1, size, TILE, LANES), kind),
        pltpu.VMEM((far_size, size, TILE, LANES), kind),
        dma(near),
        dma(near),
        dma(far),
        dma(far),
        dma(near),
        dma(near),
    ]


class Gather:
    def __init__(self, size, sources, targets, sems):
        self.size = size
        self.far = size // 2
        self.sources = sources
        self.targets = targets
        self.across_s, self.across_r, self.pair_s, self.pair_r, self.one_s, self.one_r, self.two_s, self.two_r = sems[:8]
        self.whole_s, self.whole_r, self.small_s, self.small_r, self.own = sems[8:]
        self.tensor = lax.axis_index("tensor")
        self.dp = lax.axis_index("dp")
        self.bit = self.dp % 2
        self.pair = {"dp": self.dp + 1 - 2 * self.bit, "tensor": self.tensor}
        self.near = self.tensor + 1 - 2 * (self.tensor % 2)
        self.core = {"dp": self.dp, "tensor": self.near}

    def device(self, step):
        return {"dp": self.dp, "tensor": (self.tensor + step) % self.size}

    def partners(self):
        return [self.device(s) for s in range(1, self.size)] + [self.pair]

    def slot(self, order):
        first = self.tensor if isinstance(order, int) and order % 2 == 0 else None
        if first is None:
            first = self.tensor + (order % 2) * (self.near - self.tensor)
        return (first + self.size - 2 * (order // 2)) % self.size

    def rows(self, which, part, bit):
        count = self.sources[which].shape[0] // 6
        return pl.ds((2 * part + bit) * count, count)

    def across(self, s, k):
        which, part = k // 3, k % 3
        rows = self.rows(which, part, self.bit)
        return remote(
            self.sources[which].at[rows, :],
            self.targets[which].at[self.tensor, rows, :],
            self.across_s.at[s - 1, k],
            self.across_r.at[s - 1, k],
            self.device(2 * s),
        )

    def onward(self, s, k, bit, sends, recvs, device):
        which, part = k // 3, k % 3
        rows = self.rows(which, part, bit)
        ref = self.targets[which].at[self.slot(2 * s), rows, :]
        return remote(ref, ref, sends.at[s - 1, k], recvs.at[s - 1, k], device)

    def swap(self, s, k):
        return self.onward(s, k, self.bit, self.pair_s, self.pair_r, self.pair)

    def share_one(self, s, k):
        return self.onward(s, k, self.bit, self.one_s, self.one_r, self.core)

    def share_two(self, s, k):
        return self.onward(s, k, 1 - self.bit, self.two_s, self.two_r, self.core)

    def whole(self, which):
        return remote(
            self.sources[which],
            self.targets[which].at[self.tensor],
            self.whole_s.at[which],
            self.whole_r.at[which],
            self.core,
        )

    def small(self, s, which):
        return remote(
            self.sources[which],
            self.targets[which].at[self.tensor],
            self.small_s.at[s - 1, which - 2],
            self.small_r.at[s - 1, which - 2],
            self.device(s),
        )

    def keep(self, which):
        return pltpu.make_async_copy(
            self.sources[which], self.targets[which].at[self.tensor], self.own.at[which]
        )

    def start(self):
        for which in range(4):
            self.keep(which).start()
        greet(self.partners())
        for k in range(6):
            for s in range(1, self.far):
                self.across(s, k).start()
        for which in range(2):
            self.whole(which).start()
        for s in range(1, self.size):
            for which in (2, 3):
                self.small(s, which).start()

    def forward_one(self, k):
        for s in range(1, self.far):
            self.across(s, k).wait_recv()
            self.swap(s, k).start()
            self.share_one(s, k).start()

    def forward_two(self, k):
        for s in range(1, self.far):
            self.swap(s, k).wait_recv()
            self.share_two(s, k).start()

    def arrive(self, order):
        if order == 0:
            for which in range(4):
                self.keep(which).wait()
            for s in range(1, self.size):
                for which in (2, 3):
                    self.small(s, which).wait()
        elif order == 1:
            for which in range(2):
                self.whole(which).wait()
        elif order % 2 == 1:
            for k in range(6):
                self.share_one(order // 2, k).wait_recv()
                self.share_two(order // 2, k).wait_recv()

    def finish(self):
        for s in range(1, self.far):
            for k in range(6):
                self.across(s, k).wait_send()
                self.swap(s, k).wait_send()
                self.share_one(s, k).wait_send()
                self.share_two(s, k).wait_send()


def norm_parts(values):
    center = values - jnp.mean(values, axis=-1, keepdims=True)
    root = lax.rsqrt(jnp.mean(center * center, axis=-1, keepdims=True) + norm_eps)
    return center * root, root


def norm_back(scaled, unit, root):
    return root * (
        scaled
        - jnp.mean(scaled, axis=-1, keepdims=True)
        - unit * jnp.mean(scaled * unit, axis=-1, keepdims=True)
    )


def feed_part(
    tokens,
    cotangent,
    cotangent_copy,
    out_weight,
    out_copy,
    left_s,
    right_s,
    scale_row,
    gain,
    shift,
    expand_left_t,
    expand_right,
    shrink_left_t,
    shrink_right,
    feed_scale,
    layer_out,
    layer_copy,
    grad_first_out,
    grad_context_out,
    pack,
    expand_s,
    shrink_s,
    x_s,
    normed_s,
    hidden_s,
    act_s,
    slope_s,
    branch_s,
    context_s,
    one_s,
    two_s,
    pre_s,
    gather,
):
    chunks = expand_s.shape[0]
    pieces = expand_s.shape[2] // LANES
    hidden = expand_s.shape[2]

    def part_of(order):
        if hidden == WIDTH:
            return order, slice(None), slice(None)
        place = order * hidden % WIDTH
        if isinstance(order, int):
            return order * hidden // WIDTH, slice(None), slice(place, place + hidden)
        place = pl.multiple_of(place, LANES)
        return order * hidden // WIDTH, slice(None), pl.ds(place, hidden)

    pack[...] = jnp.zeros_like(pack)

    def keep(first, values):
        for j in range(values.shape[1] // LANES):
            pack[first + j, :RANK, :] = values[:, j * LANES : (j + 1) * LANES]

    lam_one = feed_scale[0:1, :]
    lam_two = feed_scale[1:2, :]
    step = LANES
    steps = ROWS // step

    out_copy.wait()
    gather.forward_one(5)
    out_rank = dot_nt(context_s[...], left_s[...])
    out_low = (out_rank * scale_row).astype(bf16) * of_map(3)
    x_s[...] = dot_nn(context_s[...], out_weight[...]) + dot_nn(out_low, right_s[...])

    def first_norm(i, carry):
        rows = pl.ds(i * step, step)
        values = tokens[rows, :].astype(f32) + x_s[rows, :]
        x_s[rows, :] = values
        unit, root = norm_parts(values)
        normed = unit * gain[0:1, :] + shift[0:1, :]
        normed_s[rows, :] = normed
        hidden_s[rows, :] = normed.astype(bf16)
        return carry

    lax.fori_loop(0, steps, first_norm, 0)
    gather.forward_two(4)

    one_rank = dot_nt(hidden_s[...], expand_left_t[...])
    one_low = (one_rank * lam_one).astype(bf16)
    def expanded(order):
        if order == min(2, chunks - 1):
            gather.forward_two(5)
        gather.arrive(order)
        c = gather.slot(order)
        pre_s[order % 2, :, :hidden] = dot_nn(hidden_s[...], expand_s[c]) + dot_nn(one_low, expand_right[c])

    two_rank = None
    expanded(0)
    for order in range(chunks):
        if order + 1 < chunks:
            expanded(order + 1)
        pre = pre_s[order % 2, :, :hidden]
        cdf = 0.5 + 0.5 * lax.erf(pre * inverse_root_two)
        act_s[part_of(order)] = (pre * cdf).astype(bf16)
        slope_s[part_of(order)] = cdf + pre * jnp.exp(-0.5 * pre * pre) * inverse_root_tau
        c = gather.slot(order)
        part = dot_nn(act_s[part_of(order)], shrink_s[c])
        branch_s[...] = part if order == 0 else branch_s[...] + part
        part = dot_nt(act_s[part_of(order)], shrink_left_t[c])
        two_s[...] = part if order == 0 else two_s[...] + part
    two_rank = two_s[...]
    gather.finish()
    two_low = (two_rank * lam_two).astype(bf16)
    branch_s[...] += dot_nn(two_low, shrink_right[...])

    cotangent_copy.wait()

    def second_norm(i, carry):
        rows = pl.ds(i * step, step)
        unit, root = norm_parts(normed_s[rows, :] + branch_s[rows, :])
        layer_out[rows, :] = (unit * gain[1:2, :] + shift[1:2, :]).astype(bf16)
        grad = norm_back(cotangent[rows, :].astype(f32) * gain[1:2, :], unit, root)
        branch_s[rows, :] = grad
        return carry

    lax.fori_loop(0, steps, second_norm, 0)
    layer_copy.start()
    grad_branch = branch_s[...].astype(bf16)
    two_back = dot_nt(grad_branch, shrink_right[...])
    two_small = (two_back * lam_two).astype(bf16)
    two_small_t = two_small.T
    one_low_t = one_low.T
    keep(18, dot_tn(two_low, grad_branch))
    pack[24, 5:6, :RANK] = jnp.sum(two_rank * two_back, axis=0, keepdims=True)

    one_s[...] = jnp.zeros_like(one_s)

    def backward(order, carry):
        c = gather.slot(order)
        here = part_of(order)
        grad_act = dot_nt(grad_branch, shrink_s[c]) + dot_nn(two_small, shrink_left_t[c])
        grad_pre = (grad_act * slope_s[here]).astype(bf16)
        keep(SPLIT_AT + (chunks + c) * pieces, dot_nn(two_small_t, act_s[here]))
        keep(SPLIT_AT + c * pieces, dot_nn(one_low_t, grad_pre))
        branch_s[...] += dot_nt(grad_pre, expand_s[c])
        one_s[...] += dot_nt(grad_pre, expand_right[c])
        return carry

    lax.fori_loop(0, chunks, backward, 0)
    one_back = one_s[...]
    one_small = (one_back * lam_one).astype(bf16)
    branch_s[...] += dot_nn(one_small, expand_left_t[...])
    keep(12, dot_tn(one_small, hidden_s[...]))
    pack[24, 4:5, :RANK] = jnp.sum(one_rank * one_back, axis=0, keepdims=True)

    def first_back(i, carry):
        rows = pl.ds(i * step, step)
        unit, root = norm_parts(x_s[rows, :])
        grad_first_out[rows, :] = norm_back(branch_s[rows, :] * gain[0:1, :], unit, root)
        return carry

    lax.fori_loop(0, steps, first_back, 0)
    grad_attended = grad_first_out[...].astype(bf16)
    out_back = dot_nt(grad_attended, right_s[...])
    out_small = (out_back * scale_row).astype(bf16) * of_map(3)
    grad_context = dot_nt(grad_attended, out_weight[...]) + dot_nn(out_small, left_s[...])
    for p in range(PAIRS):
        grad_context_out[p] = grad_context[:, p * LANES : (p + 1) * LANES].astype(bf16)
    keep(0, dot_tn(out_small, context_s[...])[3 * TILE : 3 * TILE + RANK, :])
    keep(6, dot_tn(out_low, grad_attended)[3 * TILE : 3 * TILE + RANK, :])
    pack[24, 3:4, :STACK] = jnp.sum(out_rank * out_back, axis=0, keepdims=True)


def front_kernel(
    segment,
    live,
    tokens,
    table,
    left_t,
    right,
    scale,
    gain,
    shift,
    expand_left_t,
    shrink_right,
    feed_scale,
    mix_weight,
    cotangent,
    out_weight,
    expand,
    shrink,
    expand_right,
    shrink_left_t,
    grad_first,
    grad_context,
    pack,
    layer_to,
    q_to,
    k_to,
    v_to,
    tq_to,
    tk_to,
    tr_to,
    left_to,
    right_to,
    rank_to,
    table_rank_to,
    shares_out,
    layer_s,
    q_s,
    k_s,
    v_s,
    tq_s,
    tk_s,
    tr_s,
    left_s,
    right_s,
    rank_s,
    table_rank_s,
    mix_s,
    cotangent_s,
    out_s,
    expand_s,
    shrink_s,
    expand_right_s,
    shrink_left_s,
    shares_s,
    bias_s,
    across_s,
    x_s,
    normed_s,
    hidden_s,
    act_s,
    slope_s,
    branch_s,
    context_s,
    one_s,
    two_s,
    pre_s,
    share_sems,
    load_sems,
    keep_sems,
    *gather_sems,
):
    mix_copies = [
        pltpu.make_async_copy(mix_weight.at[i], mix_s.at[i], load_sems.at[i]) for i in range(3)
    ]
    cotangent_copy = pltpu.make_async_copy(cotangent, cotangent_s, load_sems.at[3])
    out_copy = pltpu.make_async_copy(out_weight, out_s, load_sems.at[4])
    for copy in mix_copies:
        copy.start()
    gather = Gather(
        expand_s.shape[0],
        (expand, shrink, expand_right, shrink_left_t),
        (expand_s, shrink_s, expand_right_s, shrink_left_s),
        gather_sems,
    )
    gather.start()
    cotangent_copy.start()
    out_copy.start()
    left_s[...] = jnp.zeros_like(left_s)
    right_s[...] = jnp.zeros_like(right_s)
    for a in range(4):
        left_s[a * TILE : a * TILE + RANK, :] = left_t[:, a, :]
        right_s[a * TILE : a * TILE + RANK, :] = right[:, a, :]
    scale_row = spread(scale)
    attend_part(
        segment,
        live,
        tokens,
        table,
        mix_s,
        mix_copies,
        left_s,
        right_s,
        scale_row,
        rank_s,
        table_rank_s,
        shares_out,
        q_s,
        k_s,
        v_s,
        tq_s,
        tk_s,
        tr_s,
        context_s,
        shares_s,
        bias_s,
        across_s,
        (
            (slope_s.at[0], slope_s.at[1]),
            (slope_s.at[2], slope_s.at[3]),
            (pre_s.at[0], pre_s.at[1]),
            (x_s, normed_s),
            branch_s,
        ),
        share_sems,
        gather,
    )
    kept = [
        pltpu.make_async_copy(source, target, keep_sems.at[i])
        for i, (source, target) in enumerate(
            (
                (layer_s, layer_to),
                (q_s, q_to),
                (k_s, k_to),
                (v_s, v_to),
                (tq_s, tq_to),
                (tk_s, tk_to),
                (tr_s, tr_to),
                (left_s, left_to),
                (right_s, right_to),
                (rank_s, rank_to),
                (table_rank_s, table_rank_to),
            )
        )
    ]
    for copy in kept[1:]:
        copy.start()
    feed_part(
        tokens,
        cotangent_s,
        cotangent_copy,
        out_s,
        out_copy,
        left_s,
        right_s,
        scale_row,
        gain,
        shift,
        expand_left_t,
        expand_right_s,
        shrink_left_s,
        shrink_right,
        feed_scale,
        layer_s,
        kept[0],
        grad_first,
        grad_context,
        pack,
        expand_s,
        shrink_s,
        x_s,
        normed_s,
        hidden_s,
        act_s,
        slope_s,
        branch_s,
        context_s,
        one_s,
        two_s,
        pre_s,
        gather,
    )

    def finish(p, carry):
        pltpu.make_async_copy(shares_s.at[p], shares_out.at[p], share_sems.at[p]).wait()
        return carry

    lax.fori_loop(0, PAIRS, finish, 0)
    for copy in kept:
        copy.wait()


def front(size, tiles, *args):
    hidden = args[15].shape[1]
    wide = size * hidden // WIDTH
    piece = jax.ShapeDtypeStruct((PAIRS, ROWS, LANES), bf16)
    rows = jax.ShapeDtypeStruct((ROWS, WIDTH), bf16)
    dma = pltpu.SemaphoreType.DMA
    steps = (max(size // 2 - 1, 1), 6)
    stack = jax.ShapeDtypeStruct((STACK, WIDTH), bf16)
    rank = jax.ShapeDtypeStruct((ROWS, STACK), f32)
    kept = (rows, piece, piece, piece, piece, piece, rows, stack, stack, rank, rank)
    return pl.pallas_call(
        front_kernel,
        out_shape=(
            jax.ShapeDtypeStruct((ROWS, WIDTH), f32),
            piece,
            jax.ShapeDtypeStruct((tiles, TILE, LANES), f32),
        )
        + kept
        + (jax.ShapeDtypeStruct((PAIRS, 2, ROWS, ROWS), bf16),),
        in_specs=[vmem()] * 12 + [anywhere()] * 7,
        out_specs=(vmem(),) * 3 + (anywhere(),) * 12,
        scratch_shapes=[pltpu.VMEM(array.shape, array.dtype) for array in kept]
        + [
            pltpu.VMEM((3, WIDTH, WIDTH), bf16),
            pltpu.VMEM((ROWS, WIDTH), bf16),
            pltpu.VMEM((WIDTH, WIDTH), bf16),
            pltpu.VMEM((size, WIDTH, hidden), bf16),
            pltpu.VMEM((size, hidden, WIDTH), bf16),
            pltpu.VMEM((size, RANK, hidden), bf16),
            pltpu.VMEM((size, RANK, hidden), bf16),
            pltpu.VMEM((PAIRS, 2, ROWS, ROWS), bf16),
            pltpu.VMEM((ROWS, ROWS), f32),
            pltpu.VMEM((2, 2, ROWS, ROWS), bf16),
            pltpu.VMEM((ROWS, WIDTH), f32),
            pltpu.VMEM((ROWS, WIDTH), f32),
            pltpu.VMEM((ROWS, WIDTH), bf16),
            pltpu.VMEM((wide, ROWS, WIDTH), bf16),
            pltpu.VMEM((wide, ROWS, WIDTH), f32),
            pltpu.VMEM((ROWS, WIDTH), f32),
            pltpu.VMEM((ROWS, WIDTH), bf16),
            pltpu.VMEM((ROWS, RANK), f32),
            pltpu.VMEM((ROWS, RANK), f32),
            pltpu.VMEM((2, ROWS, WIDTH), f32),
            dma((PAIRS,)),
            dma((5,)),
            dma((len(kept),)),
        ]
        + [dma(steps)] * 8
        + [dma((2,))] * 2
        + [dma((size - 1, 2))] * 2
        + [dma((4,))],
        compiler_params=pltpu.CompilerParams(
            vmem_limit_bytes=60 * 2**20, collective_id=0, has_side_effects=True
        ),
        name="front",
    )(*args)


def back_kernel(
    left_s,
    right_s,
    rank_s,
    table_rank_s,
    scale,
    early,
    grad_context_in,
    q_in,
    k_in,
    v_in,
    tq_in,
    tk_in,
    tokens_in,
    tr_in,
    mix_in,
    grad_first_in,
    shares_in,
    grad_tokens,
    early_out,
    tail_out,
    grad_context,
    q_s,
    k_s,
    v_s,
    tq_s,
    tk_s,
    tokens,
    tr_s,
    mix_weight,
    grad_first,
    shares_s,
    gl_s,
    qf_s,
    kf_s,
    gq_s,
    gk_s,
    gt_s,
    grads_s,
    tables_s,
    tail,
    sems,
    load_sems,
    *reduce_refs,
):
    arrived, crossed = reduce_refs[0], reduce_refs[1]
    groups = Groups(arrived.shape[0] // 2 + 1, crossed.shape[0] * 2)
    first = Reduction(groups, early, arrived, crossed, early_out, reduce_refs[2:8])
    second = Reduction(groups, tail, reduce_refs[8], reduce_refs[9], tail_out, reduce_refs[10:16])
    row, lane = block_iotas()
    beyond = lane >= row
    inside = (row + lane <= LANES - 1).astype(bf16)
    ends = lax.broadcasted_iota(jnp.int32, (2 * LANES, LANES), 1)
    pick_first = (ends == 0).astype(bf16)
    pick_last = (ends == LANES - 1).astype(bf16)
    flip = (row + lane == LANES - 1).astype(bf16)

    needed = [
        pltpu.make_async_copy(source, target, load_sems.at[4 + i])
        for i, (source, target) in enumerate(
            (
                (grad_context_in, grad_context),
                (v_in, v_s),
                (q_in, q_s),
                (k_in, k_s),
                (tq_in, tq_s),
                (tk_in, tk_s),
            )
        )
    ]
    for copy in needed:
        copy.start()

    def begin(p, carry):
        pltpu.make_async_copy(shares_in.at[p], shares_s.at[p], sems.at[p]).start()
        return carry

    lax.fori_loop(0, PAIRS, begin, 0)
    loads = [
        pltpu.make_async_copy(source, target, load_sems.at[i])
        for i, (source, target) in enumerate(
            (
                (tokens_in, tokens),
                (tr_in, tr_s),
                (mix_in, mix_weight),
                (grad_first_in, grad_first),
            )
        )
    ]
    greet(groups.partners())
    first.start()
    for copy in loads:
        copy.start()
    for copy in needed:
        copy.wait()
    tail[...] = jnp.zeros_like(tail)
    scale_row = spread(scale)
    low = (rank_s[...] * scale_row).astype(bf16)
    table_low = (table_rank_s[...] * scale_row).astype(bf16)

    def keep(index, values):
        for j in range(values.shape[1] // LANES):
            tail[index + j] = values[:, j * LANES : (j + 1) * LANES].astype(bf16)

    def flipped(values):
        return jnp.concatenate(
            [
                dot_nn(flip, values[b * LANES : (b + 1) * LANES, :]).astype(bf16)
                for b in range(BLOCKS)
            ],
            axis=0,
        )

    def rows_of(group):
        return [
            slice(a * LANES, (a + 1) * LANES)
            for a in range(group * BACK_GROUP, (group + 1) * BACK_GROUP)
        ]

    def grads(p, which, group):
        rows = rows_of(group)
        every = slice(rows[0].start, rows[-1].stop)
        grad = dot_nt(grad_context[p, every, :] * head_mask(which), v_s[p])
        shares = [shares_s[p, which, r, :].astype(f32) for r in rows]
        prods = [
            grad[i * LANES : (i + 1) * LANES, :] * shares[i] for i in range(BACK_GROUP)
        ]
        inner = [jnp.sum(prod, axis=1, keepdims=True) for prod in prods]
        for i, r in enumerate(rows):
            gl_s[which, r, :] = (prods[i] - shares[i] * inner[i]).astype(bf16)

    def fold(which, group, target, turn):
        rows = rows_of(group)
        turned = [
            dot_nt(flip, gl_s[which, :, r]) if turn else dot_nn(flip, gl_s[which, r, :])
            for r in rows
        ]
        for t, r in zip(turned, rows):
            target[which, r, :ROWS] = t.astype(bf16)
        for i, r in enumerate(rows):
            target[which, r, ROWS:] = fold_rows(
                turned[i], group * BACK_GROUP + i, beyond, inside, pick_first, pick_last
            ).astype(bf16)

    def close(p, which, parts):
        gc_t, k_t, q_t, tk_t, tq_t, q_rev_t, k_rev_t = parts
        half = slice(which * 64, which * 64 + 64)
        gq_t = dot_nt(jnp.concatenate([k_t[half, :], tk_t[half, :]], axis=1), qf_s[which])
        gk_t = dot_nt(jnp.concatenate([q_t[half, :], tq_t[half, :]], axis=1), kf_s[which])
        gq_s[half, :] = (gq_t * score_scale).astype(bf16)
        gk_s[half, :] = (gk_t * score_scale).astype(bf16)
        gtk = dot_nn(q_rev_t[half, :], qf_s[which, :, ROWS:])
        gtq = dot_nn(k_rev_t[half, :], kf_s[which, :, ROWS:])
        gt_s[0, half, :] = (gtq * score_scale).astype(bf16)
        gt_s[1, half, :] = (gtk * score_scale).astype(bf16)
        gt_s[2, half, :] = dot_nn(gc_t[half, :], shares_s[p, which]).astype(bf16)

    sections = BLOCKS // BACK_GROUP
    pltpu.make_async_copy(shares_in.at[0], shares_s.at[0], sems.at[0]).wait()
    for group in range(sections):
        grads(0, 0, group)

    def pair(p, carry):
        later = jnp.minimum(p + 1, PAIRS - 1)

        @pl.when(p < PAIRS - 1)
        def _():
            pltpu.make_async_copy(
                shares_in.at[later], shares_s.at[later], sems.at[later]
            ).wait()

        @pl.when(p == 2)
        def _():
            first.middle()

        @pl.when(p == 4)
        def _():
            first.last()

        parts = (
            grad_context[p].T,
            k_s[p].T,
            q_s[p].T,
            tk_s[p].T,
            tq_s[p].T,
            flipped(q_s[p]).T,
            flipped(k_s[p]).T,
        )
        for group in range(sections):
            fold(0, group, qf_s, False)
            grads(p, 1, group)
            fold(0, group, kf_s, True)
        close(p, 0, parts)
        for group in range(sections):
            fold(1, group, qf_s, False)
            grads(later, 0, group)
            fold(1, group, kf_s, True)
        close(p, 1, parts)
        lanes = pl.ds(pl.multiple_of(p * LANES, LANES), LANES)
        for b in range(BLOCKS):
            rows = slice(b * LANES, (b + 1) * LANES)
            grads_s[0, rows, lanes] = dot_nt(flip, gq_s[:, rows]).astype(bf16)
            grads_s[1, rows, lanes] = dot_nt(flip, gk_s[:, rows]).astype(bf16)
        grads_s[2, :, lanes] = gt_s[2].T
        tables_s[0, :, lanes] = gt_s[0].T
        tables_s[1, :, lanes] = gt_s[1].T
        return carry

    lax.fori_loop(0, PAIRS, pair, 0)

    for copy in loads:
        copy.wait()

    def backs(source, count):
        total = None
        lane = lax.broadcasted_iota(jnp.int32, (1, STACK), 1)
        for which in range(count):
            part = dot_nt(source[which], right_s[...])
            part = jnp.where(lane // TILE == which, part, 0.0)
            total = part if total is None else total + part
        return total

    back = backs(grads_s, 3)
    table_back = backs(tables_s, 2)
    small = (back * scale_row).astype(bf16)
    table_small = (table_back * scale_row).astype(bf16)
    left_sum = dot_tn(small, tokens[...]) + dot_tn(table_small, tr_s[...])
    low_t = low.T
    table_low_t = table_low.T
    for which in range(3):
        rows = slice(which * TILE, (which + 1) * TILE)
        right_sum = dot_nn(low_t[rows, :], grads_s[which])
        if which < 2:
            right_sum = right_sum + dot_nn(table_low_t[rows, :], tables_s[which])
        keep(which * 6, left_sum[rows, :])
        keep(18 + which * 6, right_sum)
    tail[36, :1, :STACK] = jnp.sum(
        rank_s[...] * back + table_rank_s[...] * table_back, axis=0, keepdims=True
    ).astype(bf16)
    first.finish()
    second.start()
    grad_tokens[...] = grad_first[...] + dot_nn(small, left_s[...])
    grad_tokens[...] += dot_nt(grads_s[0], mix_weight[0])
    second.middle()
    grad_tokens[...] += dot_nt(grads_s[1], mix_weight[1])
    second.last()
    grad_tokens[...] += dot_nt(grads_s[2], mix_weight[2])
    second.finish()


def back(tail_tiles, near_size, far_size, *args):
    early = args[5]
    piece = pltpu.VMEM((PAIRS, ROWS, LANES), bf16)
    return pl.pallas_call(
        back_kernel,
        out_shape=(
            jax.ShapeDtypeStruct((ROWS, WIDTH), f32),
            jax.ShapeDtypeStruct(early.shape, f32),
            jax.ShapeDtypeStruct((tail_tiles, TILE, LANES), bf16),
        ),
        in_specs=[vmem()] * 6 + [anywhere()] * 11,
        out_specs=(vmem(),) * 3,
        scratch_shapes=[piece] * 6
        + [
            pltpu.VMEM((ROWS, WIDTH), bf16),
            pltpu.VMEM((ROWS, WIDTH), bf16),
            pltpu.VMEM((3, WIDTH, WIDTH), bf16),
            pltpu.VMEM((ROWS, WIDTH), f32),
            pltpu.VMEM((PAIRS, 2, ROWS, ROWS), bf16),
            pltpu.VMEM((2, ROWS, ROWS), bf16),
            pltpu.VMEM((2, ROWS, 2 * ROWS), bf16),
            pltpu.VMEM((2, ROWS, 2 * ROWS), bf16),
            pltpu.VMEM((LANES, ROWS), bf16),
            pltpu.VMEM((LANES, ROWS), bf16),
            pltpu.VMEM((3, LANES, ROWS), bf16),
            pltpu.VMEM((3, ROWS, WIDTH), bf16),
            pltpu.VMEM((2, ROWS, WIDTH), bf16),
            pltpu.VMEM((tail_tiles, TILE, LANES), bf16),
            pltpu.SemaphoreType.DMA((PAIRS,)),
            pltpu.SemaphoreType.DMA((10,)),
        ]
        + reduction_scratch(early.shape[0], near_size, far_size, f32)
        + reduction_scratch(tail_tiles, near_size, far_size, bf16),
        compiler_params=pltpu.CompilerParams(
            vmem_limit_bytes=58 * 2**20, collective_id=1, has_side_effects=True
        ),
        name="back",
    )(*args)


def unpack_kernel(
    early,
    tail,
    tokens_in,
    layer_in,
    tokens_out,
    layer_out,
    left,
    scale,
    right,
    expand_left_t,
    expand_right,
    shrink_left_t,
    feed_scale,
    shrink_right,
    tokens_s,
    layer_s,
    sems,
):
    ins = []
    outs = []
    for i in range(4):
        rows = pl.ds(i * LANES, LANES)
        for n, (source, held, target) in enumerate(
            ((tokens_in, tokens_s, tokens_out), (layer_in, layer_s, layer_out))
        ):
            ins.append(
                pltpu.make_async_copy(source.at[rows, :], held.at[rows, :], sems.at[n, i])
            )
            outs.append(
                pltpu.make_async_copy(held.at[rows, :], target.at[rows, :], sems.at[2 + n, i])
            )
    for copy in ins:
        copy.start()
    for copy, onward in zip(ins, outs):
        copy.wait()
        onward.start()
    me = lax.axis_index("tensor")
    pieces = expand_right.shape[1] // LANES
    split = SPLIT_AT + me * pieces
    skip = (early.shape[0] - SPLIT_AT) // 2
    for j in range(WIDTH // LANES):
        lanes = slice(j * LANES, (j + 1) * LANES)
        for which in range(3):
            left[:, which, lanes] = tail[which * 6 + j, :RANK, :].astype(f32)
            right[:, which, lanes] = tail[18 + which * 6 + j, :RANK, :].astype(f32)
        left[:, 3, lanes] = early[j, :RANK, :]
        right[:, 3, lanes] = early[6 + j, :RANK, :]
        expand_left_t[:, lanes] = early[12 + j, :RANK, :]
        shrink_right[:, lanes] = early[18 + j, :RANK, :]
    total = lax.axis_size("tensor") * pieces
    for j in range(pieces):
        lanes = slice(j * LANES, (j + 1) * LANES)
        expand_right[:, lanes] = early[split + j, :RANK, :]
        shrink_left_t[:, lanes] = early[split + total + j, :RANK, :]
    mixed = tail[36].astype(f32)
    for which in range(3):
        scale[which : which + 1, :] = mixed[:1, which * TILE : which * TILE + RANK]
    other = early[24]
    scale[3:4, :] = other[3:4, 3 * TILE : 3 * TILE + RANK]
    feed_scale[...] = other[4:6, :RANK]
    for copy in outs:
        copy.wait()


def unpack(hidden, early, tail, tokens, layer):
    mats = jax.ShapeDtypeStruct((RANK, 4, WIDTH), f32)
    small = jax.ShapeDtypeStruct((RANK, WIDTH), f32)
    split = jax.ShapeDtypeStruct((RANK, hidden), f32)
    return pl.pallas_call(
        unpack_kernel,
        out_shape=(
            jax.ShapeDtypeStruct((ROWS, WIDTH), f32),
            jax.ShapeDtypeStruct((ROWS, WIDTH), bf16),
            mats,
            jax.ShapeDtypeStruct((4, RANK), f32),
            mats,
            small,
            split,
            split,
            jax.ShapeDtypeStruct((2, RANK), f32),
            small,
        ),
        in_specs=[vmem(), vmem(), anywhere(), anywhere()],
        out_specs=(anywhere(),) * 2 + (vmem(),) * 8,
        scratch_shapes=[
            pltpu.VMEM((ROWS, WIDTH), f32),
            pltpu.VMEM((ROWS, WIDTH), bf16),
            pltpu.SemaphoreType.DMA((4, 4)),
        ],
        name="unpack",
    )(early, tail, tokens, layer)


def body(
    tokens,
    segment,
    live,
    mix_weight,
    out_weight,
    position_table,
    norm_gain,
    norm_bias,
    mix_left,
    mix_scale,
    mix_right,
    expand_weight,
    expand_left,
    expand_right,
    shrink_weight,
    shrink_left,
    feed_scale,
    shrink_right,
    cotangent,
):
    tensor_size = lax.axis_size("tensor")
    near_size = tensor_size * 2
    far_size = lax.axis_size("dp") // 2
    hidden = expand_weight.shape[1]
    early_tiles = -(-(SPLIT_AT + 2 * tensor_size * hidden // LANES) // near_size) * near_size
    tail_tiles = -(-37 // near_size) * near_size
    left_t = jnp.transpose(mix_left, (2, 0, 1))
    right = jnp.transpose(mix_right, (1, 0, 2))
    grad_first, grad_context, early, layer_out, q, k, v, tq, tk, tr, *adapters, shares = front(
        tensor_size,
        early_tiles,
        segment.reshape(1, ROWS),
        live.reshape(1, ROWS),
        tokens,
        position_table,
        left_t,
        right,
        mix_scale,
        norm_gain,
        norm_bias,
        expand_left.T,
        shrink_right,
        feed_scale,
        mix_weight,
        cotangent,
        out_weight,
        expand_weight,
        shrink_weight,
        expand_right,
        shrink_left.T,
    )
    grad_tokens, early, tail = back(
        tail_tiles,
        near_size,
        far_size,
        *adapters,
        mix_scale,
        early,
        grad_context,
        q,
        k,
        v,
        tq,
        tk,
        tokens,
        tr,
        mix_weight,
        grad_first,
        shares,
    )
    (
        grad_tokens,
        layer_out,
        left,
        scale,
        right,
        expand_left,
        expand_right,
        shrink_left,
        feed_scale,
        shrink_right,
    ) = unpack(hidden, early, tail, grad_tokens, layer_out)
    return (
        layer_out,
        grad_tokens,
        jnp.transpose(left, (1, 2, 0)),
        scale,
        jnp.transpose(right, (1, 0, 2)),
        expand_left.T,
        expand_right,
        shrink_left.T,
        feed_scale,
        shrink_right,
    )


def solution(mesh):
    rows = P(("dp", "tensor"), None)
    line = P(("dp", "tensor"))
    return jax.shard_map(
        body,
        mesh=mesh,
        in_specs=(
            rows,
            line,
            line,
            P(),
            P(),
            P(),
            P(),
            P(),
            P(),
            P(),
            P(),
            P(None, "tensor"),
            P(),
            P(None, "tensor"),
            P("tensor", None),
            P("tensor", None),
            P(),
            P(),
            rows,
        ),
        out_specs=(
            rows,
            rows,
            P(),
            P(),
            P(),
            P(),
            P(None, "tensor"),
            P("tensor", None),
            P(),
            P(),
        ),
        check_vma=False,
    )
```

profile of v0, /device:TPU:0, one launch (start us, length us, event | category | flops | bytes accessed | tf_op | source)
XLA Modules:
  0.0 115.1 jit_solution(14578124746186570955)
XLA Ops:
  0.6 64.1 %front.1 = (f32[512,768]{1,0:T(8,128)}, bf16[6,512,128]{2,1,0:T(8,128)(2,1)}, f32[80,16,128]{2,1,0:T(8,128)}, bf16[512,768]{1,0:T(8,128)(2,1)}, bf16[6,512,128]{...) custom-call(s32[1,512]{1,0:T(1,128)} %bitcast.14, ...), custom_call_target="tpu_custom_call" | custom-call | tf_op jit(solution)/shard_map/front/pallas_call | solution.py:983
  64.8 45.6 %back.1 = (f32[512,768]{1,0:T(8,128)}, f32[80,16,128]{2,1,0:T(8,128)}, bf16[40,16,128]{2,1,0:T(8,128)(2,1)}) custom-call(bf16[64,768]{1,0:T(8,128)(2,1)} %get-tuple-element.38.left_s, bf16[64,768]{1,0:T(8,128)(2,1)} %get-tuple-element.39.right_s, f32[512,64]{1,0:T(8,128)} %get-tuple-element.40.rank_s, f32[512,64]{1,0:T(8,128)} %get-tuple-element.41.table_rank_s, ...), custom_call_target="tpu_custom_call" | custom-call | tf_op jit(solution)/shard_map/back/pallas_call | solution.py:1284
  110.4 4.4 %unpack.1 = (f32[512,768]{1,0:T(8,128)}, bf16[512,768]{1,0:T(8,128)(2,1)}, f32[12,4,768]{2,1,0:T(4,128)}, f32[4,12]{1,0:T(4,128)}, f32[12,4,768]{2,1,0:T(4,128)}...) custom-call(f32[80,16,128]{2,1,0:T(8,128)} %get-tuple-element.52.early,, ...), custom_call_target="tpu_custom_call" | custom-call | tf_op jit(solution)/shard_map/unpack/pallas_call | solution.py:1390
where the time goes:
time: 115 us
  Pallas kernels  114 us (99%)
    pallas_call x1, Pallas kernels, front(): pl.pallas_call(front_kernel, out_shape=(jax.ShapeDtypeStruct((ROWS, WIDTH...  64.1 us
    pallas_call x1, Pallas kernels, back(): pl.pallas_call(back_kernel, out_shape=(jax.ShapeDtypeStruct((ROWS, WIDTH)...  45.6 us
    pallas_call x1, Pallas kernels, unpack(): pl.pallas_call(unpack_kernel, out_shape=(jax.ShapeDtypeStruct((ROWS, WIDT...  4.43 us

commit v1 on v0

--- a/solution.py
+++ b/solution.py
@@ -338,13 +338,21 @@
     )
 
 
-def greet(devices):
+def hail(devices):
     barrier = pltpu.get_barrier_semaphore()
     for device in devices:
         pl.semaphore_signal(
             barrier, inc=1, device_id=device, device_id_type=pl.DeviceIdType.MESH
         )
-    pl.semaphore_wait(barrier, len(devices))
+
+
+def heard(devices):
+    pl.semaphore_wait(pltpu.get_barrier_semaphore(), len(devices))
+
+
+def greet(devices):
+    hail(devices)
+    heard(devices)
 
 
 class Groups:
@@ -432,7 +440,7 @@
     def middle(self):
         g = self.groups
         for copy in self.scatter():
-            copy.wait()
+            copy.wait_recv()
         total = self.pack[pl.ds(g.near * self.size, self.size)].astype(f32)
         for s in range(1, g.near_size):
             total = total + self.arrived[s - 1].astype(f32)
@@ -443,7 +451,7 @@
     def last(self):
         g = self.groups
         for copy in self.cross():
-            copy.wait()
+            copy.wait_recv()
         total = self.crossed[0].astype(f32)
         for s in range(1, g.far_size):
             total = total + self.crossed[s].astype(f32)
@@ -454,6 +462,8 @@
     def finish(self):
         for copy in self.gather():
             copy.wait()
+        for copy in self.scatter() + self.cross():
+            copy.wait_send()
 
 
 def reduction_scratch(tiles, near_size, far_size, kind):
@@ -1117,8 +1127,7 @@
             )
         )
     ]
-    greet(groups.partners())
-    first.start()
+    hail(groups.partners())
     for copy in loads:
         copy.start()
     for copy in needed:
@@ -1189,6 +1198,8 @@
     pltpu.make_async_copy(shares_in.at[0], shares_s.at[0], sems.at[0]).wait()
     for group in range(sections):
         grads(0, 0, group)
+    heard(groups.partners())
+    first.start()
 
     def pair(p, carry):
         later = jnp.minimum(p + 1, PAIRS - 1)

time: 115 us -> 115 us (level)
  no operation moved by 1% of the time
where the time goes in v1:
time: 115 us
  Pallas kernels  114 us (99%)
    pallas_call x1, Pallas kernels, front(): pl.pallas_call(front_kernel, out_shape=(jax.ShapeDtypeStruct((ROWS, WIDTH...  64.1 us
    pallas_call x1, Pallas kernels, back(): pl.pallas_call(back_kernel, out_shape=(jax.ShapeDtypeStruct((ROWS, WIDTH)...  45.7 us
    pallas_call x1, Pallas kernels, unpack(): pl.pallas_call(unpack_kernel, out_shape=(jax.ShapeDtypeStruct((ROWS, WIDT...  4.43 us

profile of v1, /device:TPU:0, one launch (start us, length us, event | category | flops | bytes accessed | tf_op | source)
XLA Modules:
  0.0 115.1 jit_solution(12809899955495835856)
XLA Ops:
  0.6 64.1 %front.1 = (f32[512,768]{1,0:T(8,128)}, bf16[6,512,128]{2,1,0:T(8,128)(2,1)}, f32[80,16,128]{2,1,0:T(8,128)}, bf16[512,768]{1,0:T(8,128)(2,1)}, bf16[6,512,128]{...) custom-call(s32[1,512]{1,0:T(1,128)} %bitcast.14, ...), custom_call_target="tpu_custom_call" | custom-call | tf_op jit(solution)/shard_map/front/pallas_call | solution.py:993
  64.8 45.7 %back.1 = (f32[512,768]{1,0:T(8,128)}, f32[80,16,128]{2,1,0:T(8,128)}, bf16[40,16,128]{2,1,0:T(8,128)(2,1)}) custom-call(bf16[64,768]{1,0:T(8,128)(2,1)} %get-tuple-element.38.left_s, bf16[64,768]{1,0:T(8,128)(2,1)} %get-tuple-element.39.right_s, f32[512,64]{1,0:T(8,128)} %get-tuple-element.40.rank_s, f32[512,64]{1,0:T(8,128)} %get-tuple-element.41.table_rank_s, ...), custom_call_target="tpu_custom_call" | custom-call | tf_op jit(solution)/shard_map/back/pallas_call | solution.py:1295
  110.5 4.4 %unpack.1 = (f32[512,768]{1,0:T(8,128)}, bf16[512,768]{1,0:T(8,128)(2,1)}, f32[12,4,768]{2,1,0:T(4,128)}, f32[4,12]{1,0:T(4,128)}, f32[12,4,768]{2,1,0:T(4,128)}...) custom-call(f32[80,16,128]{2,1,0:T(8,128)} %get-tuple-element.52.early,, ...), custom_call_target="tpu_custom_call" | custom-call | tf_op jit(solution)/shard_map/unpack/pallas_call | solution.py:1401
